TPU v7x, 32 devices: a whole 2x2x4 slice. The times are simulated.
32 devices in a mesh: groups: 2 (over x), dp: 16 (over z, y, core).
Axes of the slice: x: 2, y: 2, z: 4, core: 2. Of those that a mesh axis runs over, the one named last changes fastest.
Arguments:
- tokens: bfloat16 [8192, 8192], P(('groups', 'dp')), parts along dimension 0, may hold values from -6 to 6
- out_grad: bfloat16 [8192, 512], P(('groups', 'dp')), parts along dimension 0, may hold values from -2.09375 to 2.09375
- base_weight: bfloat16 [8192, 512], P('dp'), may hold values from -0.0625 to 0.0625
- adapter_in: bfloat16 [8192, 4096], P('dp', 'groups'), parts along dimension 1, may hold values from -0.0625 to 0.0625
- adapter_out: bfloat16 [512, 4096], P('dp', 'groups'), parts along dimension 1, may hold values from -0.75 to 0.75
- tenant_ids: int32 [64], P('groups'), parts along dimension 0, may hold values from 0 to 31, as said below
Outputs:
- mixed: bfloat16 [8192, 512], P(('groups', 'dp')), parts along dimension 0
- layer_input_gradient: bfloat16 [8192, 8192], P(('groups', 'dp')), parts along dimension 0
- grad_in: bfloat16 [8192, 4096], P('dp', 'groups'), parts along dimension 1
- grad_out: bfloat16 [512, 4096], P('dp', 'groups'), parts along dimension 1
There are 2 independent parts, one for each index of `groups`. A program takes and returns all parts, laid end to end along the dimension named above; an argument that names none is the same for every part. Nothing has to cross between parts.
Inputs may be any that keep to these rules, and one draw needn't show every extreme that they name: tenant_ids[s] names the adapter of window s; any adapter may be named by any number of windows, and the windows of one part may name up to 32 different adapters.
All inputs are finite; a program needn't handle non-finite values.
Results may differ from a plain program's by a relative error of at most 0.0049.
Values may be sent and summed in bfloat16 or wider, within the bound.
A program may use at most 128 MiB of HBM per device.

v0:
```python
import jax
import jax.numpy as jnp
from jax import lax
from jax.sharding import PartitionSpec as P

R = 64


adapter_scale = 2.0


def owner_sum(returned, slot_tenant, adapter_count):
    rows = returned.shape[0]
    flat = returned.reshape(rows, slot_tenant.shape[0], returned.shape[3])
    moved = jnp.transpose(flat, (1, 0, 2))
    summed = jax.ops.segment_sum(moved, slot_tenant, num_segments=adapter_count)
    return jnp.transpose(summed, (1, 0, 2)).reshape(rows, adapter_count * returned.shape[3])


def body(tokens, out_grad, base_weight, adapter_in, adapter_out, tenant_ids):
    devices = lax.axis_size("dp")
    slot_count = tenant_ids.shape[0] // devices
    token_rows = tokens.shape[0]
    seq_rows = token_rows // slot_count
    model_width = tokens.shape[1]
    out_width = out_grad.shape[1]
    in_rows = adapter_in.shape[0]
    out_rows = adapter_out.shape[0]
    adapter_count = adapter_in.shape[1] // R
    slot_tenant = tenant_ids.reshape(devices, slot_count).T.reshape(-1)
    in_table = adapter_in.reshape(in_rows, adapter_count, R)
    out_table = adapter_out.reshape(out_rows, adapter_count, R)
    in_send = jnp.take(in_table, slot_tenant, axis=1).reshape(in_rows, slot_count, devices, R)
    out_send = jnp.take(out_table, slot_tenant, axis=1).reshape(out_rows, slot_count, devices, R)
    in_got, out_got = (
        lax.all_to_all(in_send, "dp", split_axis=2, concat_axis=2, tiled=True),
        lax.all_to_all(out_send, "dp", split_axis=2, concat_axis=2, tiled=True),
    )
    token_blocks = tokens.reshape(slot_count, seq_rows, devices, in_rows)
    grad_blocks = out_grad.reshape(slot_count, seq_rows, devices, out_rows)
    low_rank_product = jnp.einsum(
        "ftsk,kfsr->ftr", token_blocks, in_got, preferred_element_type=jnp.float32
    ).astype(jnp.bfloat16)
    adapter_output = jnp.einsum(
        "ftr,jfsr->ftsj", low_rank_product, out_got, preferred_element_type=jnp.float32
    ).reshape(token_rows, out_width)
    gradient_low_rank = (
        adapter_scale
        * jnp.einsum("ftsj,jfsr->ftr", grad_blocks, out_got, preferred_element_type=jnp.float32)
    ).astype(jnp.bfloat16)
    part_in = jnp.einsum(
        "ftsk,ftr->kfsr", token_blocks, gradient_low_rank, preferred_element_type=jnp.float32
    )
    partial_output = adapter_scale * jnp.einsum(
        "ftsj,ftr->jfsr", grad_blocks, low_rank_product, preferred_element_type=jnp.float32
    )
    adapter_input_gradient = jnp.einsum(
        "ftr,kfsr->ftsk", gradient_low_rank, in_got, preferred_element_type=jnp.float32
    ).reshape(token_rows, model_width)
    back_in, back_out = (
        lax.all_to_all(part_in, "dp", split_axis=2, concat_axis=2, tiled=True),
        lax.all_to_all(partial_output, "dp", split_axis=2, concat_axis=2, tiled=True),
    )
    grad_in = owner_sum(back_in, slot_tenant, adapter_count).astype(jnp.bfloat16)
    grad_out = owner_sum(back_out, slot_tenant, adapter_count).astype(jnp.bfloat16)
    frozen_output = jnp.dot(
        tokens,
        lax.all_gather(base_weight, "dp", axis=0, tiled=True),
        preferred_element_type=jnp.float32,
    )
    frozen_input_gradient = lax.dot_general(
        out_grad,
        lax.all_gather(base_weight, "dp", axis=0, tiled=True),
        (((1,), (1,)), ((), ())),
        preferred_element_type=jnp.float32,
    )
    mixed = (frozen_output + adapter_scale * adapter_output).astype(jnp.bfloat16)
    layer_input_gradient = (frozen_input_gradient + adapter_input_gradient).astype(jnp.bfloat16)
    return (mixed, layer_input_gradient, grad_in, grad_out)


def solution(mesh):
    in_specs = (
        P(("groups", "dp"), None),
        P(("groups", "dp"), None),
        P("dp", None),
        P("dp", "groups"),
        P("dp", "groups"),
        P("groups"),
    )
    out_specs = (
        P(("groups", "dp"), None),
        P(("groups", "dp"), None),
        P("dp", "groups"),
        P("dp", "groups"),
    )
    return jax.shard_map(body, mesh=mesh, in_specs=in_specs, out_specs=out_specs, check_vma=False)
```

profile of v0, /device:TPU:31, one launch (start us, length us, event | category | flops | bytes accessed | tf_op | source)
XLA Modules:
  0.0 283.7 jit_solution(2761942067178217764)
XLA Ops:
  7.2 0.7 all-gather.2.cloned.1.call-update
  7.9 0.7 reshape.82
  8.8 1.2 reshape.83
  10.1 0.6 gather_fusion
  11.2 0.9 reshape.131
  12.1 6.3 %all-to-all-start = ((bf16[16,2,2048]{2,1,0:T(2,128)(2,1)}), bf16[16,2,2048]{2,1,0:T(2,128)(2,1)S(1)}, u32[]{:S(2)}, u32[]{:S(2)}) async-start(bf16[16,2,2048]{2,1,0:T(2,128)(2,1)} %reshape.131), calls=%async_computation | async-start | bytes 262144 | tf_op jit(solution)/shard_map/all_to_all | solution.py:37
  18.4 2.9 %copy.87 = bf16[512,2048]{0,1:T(8,128)(2,1)S(1)} copy(bf16[512,2048]{1,0:T(8,128)(2,1)} %param.9) | data formatting | bytes 4194304 | tf_op args[3]
  21.3 2.0 gather_fusion.1
  23.3 3.2 %copy_select_fusion = bf16[512,2,16,64]{0,3,1,2:T(8,128)(2,1)} fusion(bf16[512,2,16,64]{0,3,2,1:T(8,128)(2,1)} %bitcast.90, pred[2,16]{0,1:T(8,128)(4,1)S(1)} %compare_and_fusion), kind=kLoop, calls=%fused_computation.13 | loop fusion | flops 1048576 | bytes 4194336 | tf_op jit(solution)/shard_map/jit(_take)/select_n | solution.py:33
  26.6 6.0 %all-to-all-start.1 = ((bf16[512,2,16,64]{0,3,1,2:T(8,128)(2,1)}), bf16[512,2,16,64]{0,3,1,2:T(8,128)(2,1)S(1)}, u32[]{:S(2)}, u32[]{:S(2)}) async-start(bf16[512,2,16,64]{0,3,1,2:T(8,128)(2,1)} %copy_select_fusion), calls=%async_computation.1 | async-start | bytes 4194304 | tf_op jit(solution)/shard_map/all_to_all | solution.py:36
  32.8 6.1 %copy.109 = bf16[32,8,16,512]{3,2,1,0:T(8,128)(2,1)} copy(bf16[32,8,16,512]{3,1,2,0:T(8,128)(2,1)} %bitcast.94) | data formatting | bytes 8388608
  39.2 74.2 %all-to-all-done.1 = bf16[512,2,16,64]{0,3,1,2:T(8,128)(2,1)S(1)} async-done(((bf16[512,2,16,64]{0,3,1,2:T(8,128)(2,1)}), bf16[512,2,16,64]{0,3,1,2:T(8,128)(2,1)S(1)}, u32[]{:S(2)}, u32[]{:S(2)}) %all-to-all-start.1) | async-done | bytes 2097184 | tf_op jit(solution)/shard_map/all_to_all | solution.py:36
  113.3 6.8 %fusion.15 = bf16[2,64,128]{2,1,0:T(8,128)(2,1)S(1)} fusion(bf16[512,2,16,64]{0,3,1,2:T(8,128)(2,1)S(1)} %all-to-all-done.1, bf16[2,128,16,512]{3,2,1,0:T(8,128)(2,1)} %bitcast.91), kind=kOutput, calls=%fused_computation.21 | convolution fusion | flops 268451840 | bytes 6324224 | tf_op jit(solution)/shard_map/ftsk,kfsr->ftr/dot_general | solution.py:41
  120.4 1.0 reshape.133
  121.4 10.1 %all-to-all-start.3 = ((f32[16,1,4096]{2,1,0:T(1,128)}), f32[16,1,4096]{2,1,0:T(1,128)S(1)}, u32[]{:S(2)}, u32[]{:S(2)}) async-start(f32[16,1,4096]{2,1,0:T(1,128)} %reshape.133), calls=%async_computation.3 | async-start | bytes 524288 | tf_op jit(solution)/shard_map/all_to_all | solution.py:62
  131.7 7.2 %fusion.5 = f32[512,2,16,64]{0,3,2,1:T(8,128)S(1)} fusion(bf16[2,64,128,1]{2,1,3,0:T(8,128)(2,1)S(1)} %fusion.19, bf16[2,128,16,512]{3,2,1,0:T(8,128)(2,1)} %bitcast.92), kind=kOutput, calls=%fused_computation.11 | convolution fusion | flops 268435456 | bytes 8421376 | tf_op jit(solution)/shard_map/ftsk,ftr->kfsr/dot_general | solution.py:51
  138.9 2.6 copy.99
  141.5 6.0 %all-to-all-start.2 = ((f32[512,2,16,64]{0,3,1,2:T(8,128)}), f32[512,2,16,64]{0,3,1,2:T(8,128)}, u32[]{:S(2)}, u32[]{:S(2)}) async-start(f32[512,2,16,64]{0,3,1,2:T(8,128)} %copy.99), calls=%async_computation.2 | async-start | bytes 8388608 | tf_op jit(solution)/shard_map/all_to_all | solution.py:61
  147.6 4.9 %convolution_bitcast_fusion = f32[2,128,16,512]{1,3,2,0:T(8,128)} fusion(bf16[2,64,128,1]{2,1,3,0:T(8,128)(2,1)S(1)} %fusion.19, bf16[512,2,16,64]{0,3,1,2:T(8,128)(2,1)S(1)} %all-to-all-done.1), kind=kOutput, calls=%fused_computation.10 | convolution fusion | flops 268435456 | bytes 10518528 | tf_op jit(solution)/shard_map/ftr,kfsr->ftsk/dot_general | solution.py:57
  152.5 10.3 %copy.96 = f32[2,128,16,512]{3,2,1,0:T(8,128)} copy(f32[2,128,16,512]{1,3,2,0:T(8,128)} %convolution_bitcast_fusion) | data formatting | bytes 16777216 | tf_op jit(solution)/shard_map/ftr,kfsr->ftsk/transpose | solution.py:57
  162.9 14.6 %copy.111 = f32[32,8,16,512]{3,1,2,0:T(8,128)} copy(f32[32,8,16,512]{3,2,1,0:T(8,128)} %bitcast.87) | data formatting | bytes 16777216
  178.9 1.3 reduce
  181.1 2.1 scatter_fusion.1
  183.3 0.9 convert_element_type.41
  184.3 54.7 %all-to-all-done.2 = f32[512,2,16,64]{0,3,1,2:T(8,128)} async-done(((f32[512,2,16,64]{0,3,1,2:T(8,128)}), f32[512,2,16,64]{0,3,1,2:T(8,128)}, u32[]{:S(2)}, u32[]{:S(2)}) %all-to-all-start.2) | async-done | bytes 4194336 | tf_op jit(solution)/shard_map/all_to_all | solution.py:61
  239.0 4.8 %copy.100 = f32[512,2,16,64]{0,3,2,1:T(8,128)} copy(f32[512,2,16,64]{0,3,1,2:T(8,128)} %all-to-all-done.2) | data formatting | bytes 8388608 | tf_op jit(solution)/shard_map/all_to_all | solution.py:61
  243.8 2.5 broadcast_in_dim.30
  246.4 10.0 %scatter_fusion = f32[32,512,64]{1,2,0:T(8,128)} fusion(f32[32,512,64]{1,2,0:T(8,128)} %broadcast_in_dim.30, s32[32]{0:T(128)S(1)} %reshape.109, f32[32,512,64]{1,2,0:T(8,128)} %bitcast.86), kind=kCustom, calls=%fused_computation.2 | custom fusion | flops 1048576 | bytes 12583040 | tf_op jit(solution)/shard_map/scatter-add | solution.py:16
  256.3 2.5 convert_element_type.36
  258.9 2.4 copy.106
  261.2 10.3 %fusion = bf16[256,8192]{1,0:T(8,128)(2,1)} fusion(f32[256,8192]{1,0:T(8,128)} %bitcast.88, bf16[256,512]{1,0:T(8,128)(2,1)S(1)} %copy-done.1, bf16[8192,512]{1,0:T(8,128)(2,1)} %all-gather.2.cloned.1.call-done), kind=kOutput, calls=%fused_computation.5 | convolution fusion | flops 2151677952 | bytes 21233664 | tf_op jit(solution)/shard_map/dot_general | solution.py:71
  271.6 5.3 %fusion.10 = bf16[256,512]{1,0:T(8,128)(2,1)} fusion(f32[256,512]{1,0:T(8,128)S(1)} %copy.92, bf16[256,8192]{1,0:T(8,128)(2,1)} %param.6, bf16[8192,512]{1,0:T(8,128)(2,1)S(1)} %copy-done), kind=kOutput, calls=%fused_computation.17 | convolution fusion | flops 2147745792 | bytes 13369344 | tf_op jit(solution)/shard_map/dot_general | solution.py:66
  (37 shorter events, 4.2 us)
Async XLA Ops:
  7.2 254.1 %all-gather.2.cloned.1.call-start = ((), (), s32[]{:S(2)}) async-start(), calls=%async_computation.4 | async-start | bytes 8912896 | tf_op jit(solution)/shard_map/all_gather | solution.py:68
  12.1 14.5 %all-to-all-start = ((bf16[16,2,2048]{2,1,0:T(2,128)(2,1)}), bf16[16,2,2048]{2,1,0:T(2,128)(2,1)S(1)}, u32[]{:S(2)}, u32[]{:S(2)}) async-start(bf16[16,2,2048]{2,1,0:T(2,128)(2,1)} %reshape.131), calls=%async_computation | async-start | bytes 262144 | tf_op jit(solution)/shard_map/all_to_all | solution.py:37
  23.3 9.3 %copy-start.1 = (bf16[256,512]{1,0:T(8,128)(2,1)S(1)}, bf16[256,512]{1,0:T(8,128)(2,1)}, u32[]{:S(2)}) copy-start(bf16[256,512]{1,0:T(8,128)(2,1)} %param.7) | copy-start | bytes 786436
  26.6 86.7 %all-to-all-start.1 = ((bf16[512,2,16,64]{0,3,1,2:T(8,128)(2,1)}), bf16[512,2,16,64]{0,3,1,2:T(8,128)(2,1)S(1)}, u32[]{:S(2)}, u32[]{:S(2)}) async-start(bf16[512,2,16,64]{0,3,1,2:T(8,128)(2,1)} %copy_select_fusion), calls=%async_computation.1 | async-start | bytes 4194304 | tf_op jit(solution)/shard_map/all_to_all | solution.py:36
  121.4 20.1 %all-to-all-start.3 = ((f32[16,1,4096]{2,1,0:T(1,128)}), f32[16,1,4096]{2,1,0:T(1,128)S(1)}, u32[]{:S(2)}, u32[]{:S(2)}) async-start(f32[16,1,4096]{2,1,0:T(1,128)} %reshape.133), calls=%async_computation.3 | async-start | bytes 524288 | tf_op jit(solution)/shard_map/all_to_all | solution.py:62
  141.5 97.5 %all-to-all-start.2 = ((f32[512,2,16,64]{0,3,1,2:T(8,128)}), f32[512,2,16,64]{0,3,1,2:T(8,128)}, u32[]{:S(2)}, u32[]{:S(2)}) async-start(f32[512,2,16,64]{0,3,1,2:T(8,128)} %copy.99), calls=%async_computation.2 | async-start | bytes 8388608 | tf_op jit(solution)/shard_map/all_to_all | solution.py:61
  261.2 10.3 %copy-start = (bf16[8192,512]{1,0:T(8,128)(2,1)S(1)}, bf16[8192,512]{1,0:T(8,128)(2,1)}, u32[]{:S(2)}) copy-start(bf16[8192,512]{1,0:T(8,128)(2,1)} %all-gather.2.cloned.1.call-done) | copy-start | bytes 25165828
Sparse Core Ops, SparseCore 0:
  10.2 110.5 all-gather.1
where the time goes:
time: 286 us; the launch traced here: 284 us
  waiting for transfers between devices  130 us (45%)
  local copies, waits for them, and re-layouts  56.9 us (20%)
  matrix products  35.2 us (12%)
  starting transfers between devices  28.5 us (10%)
  other arithmetic  19.3 us (7%)
  between operations  14.3 us (5%)
    all_to_all x1, waiting for transfers between devices, body(): lax.all_to_all(in_send, 'dp', split_axis=2, concat_axis=2, tiled=True)  74.2 us
    all_to_all x1, waiting for transfers between devices, body(): lax.all_to_all(part_in, 'dp', split_axis=2, concat_axis=2, tiled=True)  54.7 us
    unnamed x14, local copies, waits for them, and re-layouts  28.5 us
    scatter-add x2, other arithmetic, owner_sum(): summed = jax.ops.segment_sum(moved, slot_tenant, num_segments=adapter_count)  12.1 us
    transpose x1, local copies, waits for them, and re-layouts, body(): jnp.einsum('ftr,kfsr->ftsk', gradient_low_rank, in_got, preferred_element...  10.3 us
    dot_general x1, matrix products, body(): lax.dot_general(out_grad, lax.all_gather(base_weight, 'dp', axis=0, tiled...  10.3 us
    all_to_all x1, starting transfers between devices, body(): lax.all_to_all(partial_output, 'dp', split_axis=2, concat_axis=2, tiled=T...  10.1 us
    dot_general x1, matrix products, body(): jnp.einsum('ftsk,ftr->kfsr', token_blocks, gradient_low_rank, preferred_e...  7.17 us
  transfers between devices with their start and end apart: 5, of which 2 were waited for; matrix products, arithmetic and copies ran while one was open for 34% of the time, Pallas kernels for 0%

commit v1 on v0

v1 whole, which is shorter than its diff:
```python
import functools

import jax
import jax.numpy as jnp
from jax import lax
from jax.experimental import pallas as pl
from jax.experimental.pallas import tpu as pltpu
from jax.sharding import PartitionSpec as P

R = 64
LANES = 128
adapter_scale = 2.0
f32 = jnp.float32
bf16 = jnp.bfloat16


def grid_of(n):
    chips = n // 2
    inner = 1
    while 4 * inner * inner <= chips:
        inner *= 2
    if chips % inner:
        inner = 1
    return chips // inner, inner


def dot(a, b, ca, cb):
    return lax.dot_general(a, b, (((ca,), (cb,)), ((), ())), preferred_element_type=f32)


def step_kernel(
    n, kr, ob, wide, small,
    keys, x, g, w, a, b,
    mixed, dx, gin, gout,
    wbuf, asend, abuf, bsend, bbuf, psend, pback, osend, gcat, lowf, frozen, total,
    wz_s, wy_s, wc_s, w_r, a_s, a_r, b_s, b_r, p_s, p_r, o_s, o_r,
):
    Z, Y = grid_of(n)
    me = lax.axis_index("dp")
    z, y, c = me // (2 * Y), (me // 2) % Y, me % 2
    rows = g.shape[0]
    half = rows // 2

    def at(zz, yy, cc):
        return (zz * Y + yy) * 2 + cc

    partner = at(z, y, 1 - c)

    def remote(src, dst, ss, rs, peer):
        return pltpu.make_async_remote_copy(
            src_ref=src, dst_ref=dst, send_sem=ss, recv_sem=rs,
            device_id={"dp": peer}, device_id_type=pl.DeviceIdType.MESH,
        )

    def peer_of(k):
        return lax.rem(me + k, n)

    def x_block(e):
        if wide:
            return x[:, pl.ds(pl.multiple_of(e * kr, kr), kr)]
        return x[e]

    barrier = pltpu.get_barrier_semaphore()

    def greet(k, carry):
        pl.semaphore_signal(
            barrier, inc=1, device_id={"dp": peer_of(k)}, device_id_type=pl.DeviceIdType.MESH
        )
        return carry

    lax.fori_loop(1, n, greet, 0)
    wbuf[me] = w[...]
    pl.semaphore_wait(barrier, n - 1)

    def w_copy(e, ss, peer):
        return remote(wbuf.at[e], wbuf.at[e], ss, w_r.at[e], peer)

    def w_right(zp):
        return w_copy(at(zp, y, c), wz_s.at[0, zp], at(z + 1, y, c))

    def w_left(zp):
        return w_copy(at(zp, y, c), wz_s.at[1, zp], at(z - 1, y, c))

    def w_side(zp, j):
        return w_copy(at(zp, y, c), wy_s.at[zp, j - 1], at(z, lax.rem(y + j, Y), c))

    def w_core(zp, yp):
        return w_copy(at(zp, yp, c), wc_s.at[zp * Y + yp], partner)

    def w_arrived(e):
        w_copy(e, wc_s.at[0], partner).wait_recv()

    def w_spread(zp):
        for j in range(1, Y):
            w_side(zp, j).start()
        w_core(zp, y).start()

    @pl.when(z < Z - 1)
    def _():
        w_right(z).start()

    @pl.when(z > 0)
    def _():
        w_left(z).start()

    w_spread(z)

    def w_hop(d):
        @pl.when(z - d >= 0)
        def _():
            w_arrived(at(z - d, y, c))

            @pl.when(z < Z - 1)
            def _():
                w_right(z - d).start()

            w_spread(z - d)

        @pl.when(z + d < Z)
        def _():
            w_arrived(at(z + d, y, c))

            @pl.when(z > 0)
            def _():
                w_left(z + d).start()

            w_spread(z + d)

    pick_step = min(2048, a.shape[1])

    def named(e, off, size):
        name = lax.broadcasted_iota(jnp.int32, (size, LANES), 0) + off
        return jnp.where(name == keys[pl.ds(e, 1), :], 1.0, 0.0).astype(bf16)

    def pick(e):
        if pick_step == a.shape[1]:
            sel = named(e, 0, pick_step)
            return [dot(r[...], sel, 1, 0).astype(bf16) for r in ((b, a) if small else (a,))]
        total[:, :LANES] = jnp.zeros((kr, LANES), f32)

        def block(j, carry):
            off = pl.multiple_of(j * pick_step, pick_step)
            total[:, :LANES] += dot(a[:, pl.ds(off, pick_step)], named(e, off, pick_step), 1, 0)
            return carry

        lax.fori_loop(0, a.shape[1] // pick_step, block, 0)
        return [total[:, :LANES].astype(bf16)]

    def a_copy(e, slot):
        return remote(asend.at[e], abuf.at[slot], a_s.at[e], a_r.at[slot], e)

    def b_copy(e, slot):
        return remote(bsend.at[e], bbuf.at[slot], b_s.at[e], b_r.at[slot], e)

    def send_a(k, carry):
        e = peer_of(k)
        picked = pick(e)
        if small:
            bsend[e] = picked[0]
            b_copy(e, me).start()
        asend[e] = picked[-1]
        a_copy(e, me).start()
        return carry

    cut = n // 2
    lax.fori_loop(1, cut, send_a, 0)
    w_hop(1)
    lax.fori_loop(cut, n, send_a, 0)
    picked = pick(me)
    if small:
        bbuf[me] = picked[0]
    abuf[me] = picked[-1]

    row = lax.broadcasted_iota(jnp.int32, (rows, LANES), 0)
    col = lax.broadcasted_iota(jnp.int32, (rows, LANES), 1)
    own = (row < half) == (col < R)

    def wait_b(k, carry):
        e = peer_of(k)
        b_copy(e, e).wait()
        return carry

    if small:
        lax.fori_loop(1, n, wait_b, 0)
        up = bbuf[...].reshape(n * ob, LANES)
    else:
        up = b[...]
    width = g.shape[1]
    low_grad = jnp.where(own, adapter_scale * dot(g[...], up, 1, 0), 0.0).astype(bf16)
    gcat[:, :width] = g[...]
    gcat[:, width:] = low_grad

    def term_in(e):
        return dot(x_block(e), gcat[:, width:], 0, 0).astype(bf16)

    def p_copy(e, slot):
        return remote(psend.at[e], pback.at[slot, pl.ds(0, kr)], p_s.at[e], p_r.at[slot], e)

    def send_p(k, carry):
        e = peer_of(k)
        psend[e] = term_in(e)
        p_copy(e, me).start()
        return carry

    if Z > 2:
        w_hop(2)
    lax.fori_loop(1, cut, send_p, 0)
    for d in range(3, Z):
        w_hop(d)
    lax.fori_loop(cut, n, send_p, 0)
    pback[me, :kr] = term_in(me)

    for j in range(1, Y):
        ys = lax.rem(y + j, Y)
        for dz in range(Z):
            zp = lax.rem(z + dz, Z)
            w_arrived(at(zp, ys, c))
            w_core(zp, ys).start()

    lowf[...] = dot(x_block(me), abuf[me], 1, 0)

    def low_step(k, carry):
        e = peer_of(k)
        a_copy(e, e).wait()
        lowf[...] += dot(x_block(e), abuf[e], 1, 0)
        return carry

    lax.fori_loop(1, n, low_step, 0)
    low = jnp.where(own, lowf[...], 0.0).astype(bf16)
    term_out = (adapter_scale * dot(g[...], low, 0, 0)).astype(bf16)

    def o_copy(e, slot):
        src = osend.at[pl.ds(pl.multiple_of(e * ob, ob), ob)]
        return remote(src, pback.at[slot, pl.ds(kr, ob)], o_s.at[e], o_r.at[slot], e)

    def send_o(k, carry):
        e = peer_of(k)
        o_copy(e, me).start()
        return carry

    if small:
        osend[...] = term_out
        lax.fori_loop(1, n, send_o, 0)
        pback[me, kr:] = osend[pl.ds(pl.multiple_of(me * ob, ob), ob), :]
    else:
        gout[...] = term_out
    frozen[...] = adapter_scale * dot(low, up, 1, 1)

    for zp in range(Z):
        for yp in range(Y):
            w_arrived(at(zp, yp, 1 - c))

    def base_step(k, carry):
        e = peer_of(k)
        frozen[...] += dot(x_block(e), wbuf[e], 1, 0)
        both = jnp.concatenate([wbuf[e], abuf[e]], axis=1)
        value = dot(gcat[...], both, 1, 1).astype(bf16)
        if wide:
            dx[:, pl.ds(pl.multiple_of(e * kr, kr), kr)] = value
        else:
            dx[e] = value
        return carry

    lax.fori_loop(0, n, base_step, 0)
    mixed[...] = frozen[...].astype(bf16)

    step = min(512, total.shape[1])
    blocks = total.shape[1] // step
    total[...] = jnp.zeros_like(total)

    def own_sum(e):
        def block(j, carry):
            off = pl.multiple_of(j * step, step)
            total[:, pl.ds(off, step)] += dot(pback[e], named(e, off, step), 1, 1)
            return carry

        lax.fori_loop(0, blocks, block, 0)

    own_sum(me)

    def sum_step(k, carry):
        e = peer_of(k)
        p_copy(e, e).wait()
        if small:
            o_copy(e, e).wait()
        own_sum(e)
        return carry

    lax.fori_loop(1, n, sum_step, 0)
    gin[...] = total[:kr, :].astype(bf16)
    if small:
        gout[...] = total[kr:, :].astype(bf16)

    for zp in range(Z):
        @pl.when((zp <= z) & (z < Z - 1))
        def _(zp=zp):
            w_right(zp).wait_send()

        @pl.when((zp >= z) & (z > 0))
        def _(zp=zp):
            w_left(zp).wait_send()

        for j in range(1, Y):
            w_side(zp, j).wait_send()
        for yp in range(Y):
            w_core(zp, yp).wait_send()


def body(tokens, out_grad, base_weight, adapter_in, adapter_out, tenant_ids):
    n = lax.axis_size("dp")
    rows, depth = tokens.shape
    width = out_grad.shape[1]
    kr = adapter_in.shape[0]
    orows = adapter_out.shape[0]
    columns = adapter_in.shape[1]
    wide = kr % LANES == 0
    small = orows % 16 == 0
    ob = orows if small else 16
    slots = tenant_ids.shape[0] // n
    assert slots * R == LANES
    Z, Y = grid_of(n)

    keys = (tenant_ids[:, None] * R + jnp.arange(R, dtype=jnp.int32)[None, :]).reshape(n, LANES)
    if wide:
        x, dx_shape = tokens, (rows, depth)
    else:
        x = tokens.reshape(rows, n, kr).transpose(1, 0, 2)
        dx_shape = (n, rows, kr)
    if small:
        b, gout_shape = adapter_out, (orows, columns)
    else:
        table = adapter_out.reshape(orows, columns // R, R)
        sent = jnp.take(table, tenant_ids, axis=1).reshape(orows, n, LANES).transpose(1, 0, 2)
        b = lax.all_to_all(sent, "dp", split_axis=0, concat_axis=0, tiled=True).reshape(width, LANES)
        gout_shape = (width, LANES)
    vmem = pl.BlockSpec(memory_space=pltpu.VMEM)
    dma = pltpu.SemaphoreType.DMA
    trows = kr + ob if small else kr
    mixed, dx, grad_in, out_part = pl.pallas_call(
        functools.partial(step_kernel, n, kr, ob, wide, small),
        out_shape=(
            jax.ShapeDtypeStruct((rows, width), bf16),
            jax.ShapeDtypeStruct(dx_shape, bf16),
            jax.ShapeDtypeStruct((kr, columns), bf16),
            jax.ShapeDtypeStruct(gout_shape, bf16),
        ),
        in_specs=[vmem] * 6,
        out_specs=[vmem] * 4,
        scratch_shapes=[
            pltpu.VMEM((n, kr, width), bf16),
            pltpu.VMEM((n, kr, LANES), bf16),
            pltpu.VMEM((n, kr, LANES), bf16),
            pltpu.VMEM((n, ob, LANES), bf16),
            pltpu.VMEM((n, ob, LANES), bf16),
            pltpu.VMEM((n, kr, LANES), bf16),
            pltpu.VMEM((n, trows, LANES), bf16),
            pltpu.VMEM((n * ob, LANES), bf16),
            pltpu.VMEM((rows, width + LANES), bf16),
            pltpu.VMEM((rows, LANES), f32),
            pltpu.VMEM((rows, width), f32),
            pltpu.VMEM((trows, columns), f32),
            dma((2, Z)), dma((Z, max(Y - 1, 1))), dma((Z * Y,)), dma((n,)),
            dma((n,)), dma((n,)), dma((n,)), dma((n,)),
            dma((n,)), dma((n,)), dma((n,)), dma((n,)),
        ],
        compiler_params=pltpu.CompilerParams(
            collective_id=0, has_side_effects=True, vmem_limit_bytes=58 * 1024 * 1024
        ),
        cost_estimate=pl.CostEstimate(
            flops=8 * rows * depth * (width + LANES), bytes_accessed=8 * rows * depth, transcendentals=0
        ),
    )(keys, x, out_grad, base_weight, adapter_in, b)
    if not wide:
        dx = dx.transpose(1, 0, 2).reshape(rows, depth)
    if small:
        grad_out = out_part
    else:
        got = lax.all_to_all(
            out_part.reshape(n, orows, LANES), "dp", split_axis=0, concat_axis=0, tiled=True
        )
        moved = got.reshape(n, orows, slots, R).transpose(0, 2, 1, 3).reshape(n * slots, orows, R)
        summed = jax.ops.segment_sum(
            moved.astype(f32), tenant_ids, num_segments=columns // R
        )
        grad_out = summed.transpose(1, 0, 2).reshape(orows, columns).astype(bf16)
    return mixed, dx, grad_in, grad_out


def solution(mesh):
    in_specs = (
        P(("groups", "dp"), None),
        P(("groups", "dp"), None),
        P("dp", None),
        P("dp", "groups"),
        P("dp", "groups"),
        P("groups"),
    )
    out_specs = (
        P(("groups", "dp"), None),
        P(("groups", "dp"), None),
        P("dp", "groups"),
        P("dp", "groups"),
    )
    return jax.shard_map(body, mesh=mesh, in_specs=in_specs, out_specs=out_specs, check_vma=False)
```

time: 286 us -> 180 us (0.63)
  Pallas kernels: 0 us -> 167 us
  waiting for transfers between devices: 130 us -> 0 us
  local copies, waits for them, and re-layouts: 56.9 us -> 8.77 us
  matrix products: 35.2 us -> 0 us
  starting transfers between devices: 28.5 us -> 0 us
  other arithmetic: 19.3 us -> 1.27 us
  between operations: 14.3 us -> 0.65 us
    pallas_call x0 -> x1, Pallas kernels: none -> 167 us  [body(): pl.pallas_call(functools.partial(step_kernel, n, kr, ob, wide, small), ou...]
    all_to_all x4 -> x0, waiting for transfers between devices: 129 us -> none  [the longest x1 74.2 us: body(): lax.all_to_all(in_send, 'dp', split_axis=2, concat_axis=2, tiled=True)]
    dot_general x7 -> x0, matrix products: 35 us -> none  [the longest x1 10.3 us: body(): lax.dot_general(out_grad, lax.all_gather(base_weight, 'dp', axis=0, tiled...]
    all_to_all x4 -> x0, starting transfers between devices: 28.5 us -> none  [the longest x1 10.1 us: body(): lax.all_to_all(partial_output, 'dp', split_axis=2, concat_axis=2, tiled=T...]
    unnamed x14 -> x8, local copies, waits for them, and re-layouts: 28.5 us -> 8.44 us
    transpose x4 -> x0, local copies, waits for them, and re-layouts: 13.3 us -> none  [the longest x1 10.3 us: body(): jnp.einsum('ftr,kfsr->ftsk', gradient_low_rank, in_got, preferred_element...]
    scatter-add x2 -> x0, other arithmetic: 12.1 us -> none  [owner_sum(): summed = jax.ops.segment_sum(moved, slot_tenant, num_segments=adapter_count)]
    all_to_all x3 -> x0, local copies, waits for them, and re-layouts: 5.66 us -> none  [the longest x1 4.84 us: body(): lax.all_to_all(part_in, 'dp', split_axis=2, concat_axis=2, tiled=True)]
  transfers between devices with their start and end apart: 5 -> 0, of which waited for: 2 -> 0; matrix products, arithmetic and copies ran while one was open for 34% -> 0% of each run, Pallas kernels for 0% -> 0%
where the time goes in v1:
time: 180 us; the launch traced here: 177 us
  Pallas kernels  167 us (93%)
  local copies, waits for them, and re-layouts  8.77 us (5%)
    pallas_call x1, Pallas kernels, body(): pl.pallas_call(functools.partial(step_kernel, n, kr, ob, wide, small), ou...  167 us
    unnamed x8, local copies, waits for them, and re-layouts  8.44 us

profile of v1, /device:TPU:31, one launch (start us, length us, event | category | flops | bytes accessed | tf_op | source)
XLA Modules:
  0.0 177.4 jit_solution(6745437710805470591)
XLA Ops:
  0.6 0.7 broadcast_multiply_fusion
  1.3 0.1 add.26
  1.4 0.1 add.22
  1.5 0.1 add.23
  1.5 0.1 add.24
  1.6 0.6 broadcast_add_fusion.keys
  2.2 166.7 %shard_map.93 = (bf16[256,512]{1,0:T(8,128)(2,1)}, bf16[256,8192]{1,0:T(8,128)(2,1)}, bf16[512,2048]{1,0:T(8,128)(2,1)}, bf16[32,2048]{1,0:T(8,128)(2,1)}) custom-call(s32[16,128]{1,0:T(8,128)} %broadcast_add_fusion.keys, bf16[256,8192]{1,0:T(8,128)(2,1)} %x.1, bf16[256,512]{1,0:T(8,128)(2,1)} %g.1, bf16[512,512]{1,0:T(8,128)(2,1)} %w.1, ...), custom_call_target="tpu_custom_call" | custom-call | flops 10737418240 | bytes 16777216 | tf_op jit(solution)/shard_map/pallas_call | solution.py:339
  168.9 1.7 copy.14
  170.6 0.0 copy-start
  170.6 4.8 %copy.15 = bf16[256,8192]{1,0:T(8,128)(2,1)} copy(bf16[256,8192]{1,0:T(8,128)(2,1)} %get-tuple-element.9) | data formatting | bytes 8388608
  175.4 0.0 copy-done
  175.4 0.0 copy-start.1
  175.4 1.3 copy.16
  176.7 0.0 copy-done.1
  176.7 0.7 copy.17
  (1 shorter events, 0.0 us)
Async XLA Ops:
  170.6 4.8 %copy-start = (bf16[512,2048]{1,0:T(8,128)(2,1)S(1)}, bf16[512,2048]{1,0:T(8,128)(2,1)}, u32[]{:S(2)}) copy-start(bf16[512,2048]{1,0:T(8,128)(2,1)} %get-tuple-element.10) | copy-start | bytes 6291460
  175.4 1.3 copy-start.1

commit v2 on v1

--- a/solution.py
+++ b/solution.py
@@ -53,7 +53,12 @@
         )
 
     def peer_of(k):
-        return lax.rem(me + k, n)
+        p = (k + n - 1) % n
+        q, r = p // (2 * Y), p % (2 * Y)
+        far = (q + 1) // 2
+        dz = Z // 2 + far - 2 * far * (q % 2)
+        r = (r + 1) % (2 * Y)
+        return at((z + dz + Z) % Z, (y + r // 2) % Y, (c + r % 2) % 2)
 
     def x_block(e):
         if wide:
@@ -162,10 +167,12 @@
         a_copy(e, me).start()
         return carry
 
-    cut = n // 2
-    lax.fori_loop(1, cut, send_a, 0)
-    w_hop(1)
-    lax.fori_loop(cut, n, send_a, 0)
+    hops = max(Z - 1, 1)
+    cuts = [1 + (n - 1) * d // hops for d in range(hops + 1)]
+    for d in range(1, hops):
+        lax.fori_loop(cuts[d - 1], cuts[d], send_a, 0)
+        w_hop(d)
+    lax.fori_loop(cuts[hops - 1], n, send_a, 0)
     picked = pick(me)
     if small:
         bbuf[me] = picked[0]
@@ -202,14 +209,8 @@
         p_copy(e, me).start()
         return carry
 
-    if Z > 2:
-        w_hop(2)
-    lax.fori_loop(1, cut, send_p, 0)
-    for d in range(3, Z):
-        w_hop(d)
-    lax.fori_loop(cut, n, send_p, 0)
-    pback[me, :kr] = term_in(me)
-
+    w_hop(Z - 1)
+    lax.fori_loop(1, n // 2, send_p, 0)
     for j in range(1, Y):
         ys = lax.rem(y + j, Y)
         for dz in range(Z):
@@ -217,6 +218,8 @@
             w_arrived(at(zp, ys, c))
             w_core(zp, ys).start()
 
+    lax.fori_loop(n // 2, n, send_p, 0)
+    pback[me, :kr] = term_in(me)
     lowf[...] = dot(x_block(me), abuf[me], 1, 0)
 
     def low_step(k, carry):
@@ -268,25 +271,32 @@
     blocks = total.shape[1] // step
     total[...] = jnp.zeros_like(total)
 
-    def own_sum(e):
+    group = min(4, n)
+
+    def sum_step(i, carry):
+        peers = [peer_of(i * group + k) for k in range(group)]
+
+        def arrived(e):
+            p_copy(e, e).wait()
+            if small:
+                o_copy(e, e).wait()
+
+        for k, e in enumerate(peers):
+            if k == 0:
+                pl.when(i > 0)(functools.partial(arrived, e))
+            else:
+                arrived(e)
+        terms = jnp.concatenate([pback[e] for e in peers], axis=1)
+
         def block(j, carry):
             off = pl.multiple_of(j * step, step)
-            total[:, pl.ds(off, step)] += dot(pback[e], named(e, off, step), 1, 1)
+            sel = jnp.concatenate([named(e, off, step) for e in peers], axis=1)
+            total[:, pl.ds(off, step)] += dot(terms, sel, 1, 1)
             return carry
 
-        lax.fori_loop(0, blocks, block, 0)
-
-    own_sum(me)
-
-    def sum_step(k, carry):
-        e = peer_of(k)
-        p_copy(e, e).wait()
-        if small:
-            o_copy(e, e).wait()
-        own_sum(e)
-        return carry
-
-    lax.fori_loop(1, n, sum_step, 0)
+        return lax.fori_loop(0, blocks, block, carry)
+
+    lax.fori_loop(0, n // group, sum_step, 0)
     gin[...] = total[:kr, :].astype(bf16)
     if small:
         gout[...] = total[kr:, :].astype(bf16)

time: 180 us -> 157 us (0.87); the launches traced: 177 us -> 157 us
  Pallas kernels: 167 us -> 146 us
    pallas_call x1, Pallas kernels: 167 us -> 146 us  [body(): pl.pallas_call(functools.partial(step_kernel, n, kr, ob, wide, small), ou...]
where the time goes in v2:
time: 157 us
  Pallas kernels  146 us (93%)
  local copies, waits for them, and re-layouts  8.77 us (6%)
    pallas_call x1, Pallas kernels, body(): pl.pallas_call(functools.partial(step_kernel, n, kr, ob, wide, small), ou...  146 us
    unnamed x8, local copies, waits for them, and re-layouts  8.44 us

profile of v2, /device:TPU:31, one launch (start us, length us, event | category | flops | bytes accessed | tf_op | source)
XLA Modules:
  0.0 157.1 jit_solution(10515523285225547729)
XLA Ops:
  0.6 0.7 broadcast_multiply_fusion
  1.3 0.1 add.26
  1.4 0.1 add.22
  1.5 0.1 add.23
  1.5 0.1 add.24
  1.6 0.6 broadcast_add_fusion.keys
  2.2 146.4 %shard_map.93 = (bf16[256,512]{1,0:T(8,128)(2,1)}, bf16[256,8192]{1,0:T(8,128)(2,1)}, bf16[512,2048]{1,0:T(8,128)(2,1)}, bf16[32,2048]{1,0:T(8,128)(2,1)}) custom-call(s32[16,128]{1,0:T(8,128)} %broadcast_add_fusion.keys, bf16[256,8192]{1,0:T(8,128)(2,1)} %x.1, bf16[256,512]{1,0:T(8,128)(2,1)} %g.1, bf16[512,512]{1,0:T(8,128)(2,1)} %w.1, ...), custom_call_target="tpu_custom_call" | custom-call | flops 10737418240 | bytes 16777216 | tf_op jit(solution)/shard_map/pallas_call | solution.py:349
  148.6 1.7 %copy.14 = bf16[256,512]{1,0:T(8,128)(2,1)} copy(bf16[256,512]{1,0:T(8,128)(2,1)} %get-tuple-element.8) | data formatting | bytes 524288
  150.3 0.0 copy-start
  150.3 4.8 %copy.15 = bf16[256,8192]{1,0:T(8,128)(2,1)} copy(bf16[256,8192]{1,0:T(8,128)(2,1)} %get-tuple-element.9) | data formatting | bytes 8388608
  155.1 0.0 copy-done
  155.1 0.0 copy-start.1
  155.1 1.3 copy.16
  156.4 0.0 copy-done.1
  156.4 0.7 copy.17
  (1 shorter events, 0.0 us)
Async XLA Ops:
  150.3 4.8 %copy-start = (bf16[512,2048]{1,0:T(8,128)(2,1)S(1)}, bf16[512,2048]{1,0:T(8,128)(2,1)}, u32[]{:S(2)}) copy-start(bf16[512,2048]{1,0:T(8,128)(2,1)} %get-tuple-element.10) | copy-start | bytes 6291460
  155.1 1.3 copy-start.1
